TPU v7x, 256 devices: a whole 4x4x8 slice. The times are simulated.
256 devices in a mesh: dom: 128 (over x, z, y), feat: 2 (over core).
Axes of the slice: x: 4, y: 4, z: 8, core: 2. Of those that a mesh axis runs over, the one named last changes fastest.
Arguments:
- node_lat: bfloat16 [131072, 512], P('dom'), may hold values from -6 to 6
- edge_lat: bfloat16 [262144, 512], P(('dom', 'feat')), may hold values from -6 to 6
- edge_src: int32 [262144], P(('dom', 'feat')), may hold values from 0 to 1535
- edge_dst: int32 [262144], P(('dom', 'feat')), may hold values from 0 to 1023
- halo_rows: int32 [1024, 64], P('dom'), may hold values from 0 to 1023
- probe_rows: int32 [2048, 128], P(('dom', 'feat')), may hold values from 0 to 1023
- probe_slot: int32 [131072, 8], P(('dom', 'feat')), may hold values from 0 to 1023
- probe_wgt: float32 [131072, 8], P(('dom', 'feat')), may hold values from 0.05 to 0.3
- probe_embed: bfloat16 [131072, 512], P(('dom', 'feat')), may hold values from -6 to 6
- edge_first: bfloat16 [2, 1536, 512], replicated, may hold values from -0.15625 to 0.15625
- edge_second: bfloat16 [2, 512, 512], replicated, may hold values from -0.25 to 0.25
- node_first: bfloat16 [2, 1024, 512], replicated, may hold values from -0.1875 to 0.1875
- node_second: bfloat16 [2, 512, 512], replicated, may hold values from -0.25 to 0.25
- decode_first: bfloat16 [512, 512], replicated, may hold values from -0.25 to 0.25
- decode_second: bfloat16 [4, 512], replicated, may hold values from -0.25 to 0.25
Outputs:
- surface_out: bfloat16 [131072, 512], P('dom')
- fields: float32 [4, 131072], P(None, ('dom', 'feat'))
All inputs are finite; a program needn't handle non-finite values.
Results may differ from a plain program's by a relative error of at most 0.013.
Values may be sent and summed in bfloat16 or wider, within the bound.
A program may use at most 64 MiB of HBM per device.

v0:
```python
import functools

import jax
import jax.numpy as jnp
from jax import lax
from jax.experimental import pallas as pl
from jax.experimental.pallas import tpu as pltpu
from jax.sharding import PartitionSpec as P

SPAN = 4
BF = jnp.bfloat16
F32 = jnp.float32
MESH = pl.DeviceIdType.MESH
OFFSETS = (1, -1, SPAN, -SPAN, SPAN + 1, -SPAN - 1, SPAN - 1, 1 - SPAN)
ROWS = 256


def dot(a, b):
    return jnp.dot(a, b, preferred_element_type=F32)


def layer_norm(values):
    centre = jnp.mean(values, axis=-1, keepdims=True)
    shifted = values - centre
    spread = jnp.mean(shifted * shifted, axis=-1, keepdims=True)
    return shifted * lax.rsqrt(spread + 1e-05)


def tiles(count, body):
    def step(i, carry):
        body(pl.multiple_of(i * ROWS, ROWS))
        return carry

    lax.fori_loop(0, count // ROWS, step, 0)


def column(row):
    return jnp.transpose(jnp.broadcast_to(row, (128, 128)))


def kernel(
    node_hbm, edge_hbm, esrc, edst, hrows, prows, pslot, pwgt, emb_hbm,
    ef_hbm, es_hbm, nf_hbm, ns_hbm, d1_hbm, d2,
    out_hbm, fields,
    h0, h1, h2, edge, emb, ef, es, nf, ns, d1,
    csrc, cdst, chalo, cprobe, ssrc, sdst, tdst, shalo, sprobe, wint,
    own, pre, hn, part, part_in, halo_out, halo_in, probe_out, probe_in,
    load_sem, store_sem, hs_sem, hr_sem, xs_sem, xr_sem, ps_sem, pr_sem,
):
    nodes, edges = h0.shape[0], edge.shape[0]
    halos, requests, probes = halo_in.shape[1], probe_in.shape[0], emb.shape[0]
    hslot, qslot = halos // 8, requests // 8
    count = lax.axis_size("dom")
    dom, feat = lax.axis_index("dom"), lax.axis_index("feat")
    peer = 1 - feat
    targets = [lax.rem(dom + off + count, count) for off in OFFSETS]

    pairs = [
        (node_hbm, h0), (edge_hbm, edge),
        (ef_hbm.at[0], ef.at[0]), (nf_hbm.at[0], nf.at[0]), (es_hbm.at[0], es.at[0]), (ns_hbm.at[0], ns.at[0]),
        (ef_hbm.at[1], ef.at[1]), (nf_hbm.at[1], nf.at[1]), (es_hbm.at[1], es.at[1]), (ns_hbm.at[1], ns.at[1]),
        (emb_hbm, emb), (d1_hbm, d1),
    ]
    loads = [pltpu.make_async_copy(src, dst, load_sem.at[i]) for i, (src, dst) in enumerate(pairs)]
    for load in loads:
        load.start()

    barrier = pltpu.get_barrier_semaphore()
    for target in targets:
        pl.semaphore_signal(barrier, inc=1, device_id=(target, feat), device_id_type=MESH)
    pl.semaphore_signal(barrier, inc=1, device_id=(dom, peer), device_id_type=MESH)

    for j in range(edges // 128):
        csrc[j * 128 : (j + 1) * 128, :] = column(esrc[j : j + 1, :])
        cdst[j * 128 : (j + 1) * 128, :] = column(edst[j : j + 1, :])
    for j in range(requests // 128):
        cprobe[j * 128 : (j + 1) * 128, :] = column(prows[j : j + 1, :])
    for j in range(halos // 128):
        pair = jnp.concatenate([hrows[2 * j : 2 * j + 1, :], hrows[2 * j + 1 : 2 * j + 2, :]], axis=1)
        chalo[j * 128 : (j + 1) * 128, :] = column(pair)

    lanes = lax.broadcasted_iota(jnp.int32, (ROWS, 128), 1)
    sublanes = lax.broadcasted_iota(jnp.int32, (ROWS, 128), 0)

    def select(out, col, r):
        here = col[pl.ds(r, ROWS), :]
        for j in range(out.shape[1] // 128):
            hit = jnp.where(here == lanes + j * 128, 1.0, 0.0).astype(BF)
            out[pl.ds(r, ROWS), j * 128 : (j + 1) * 128] = hit

    tiles(halos, lambda r: select(shalo, chalo, r))
    loads[0].wait()

    def gather_halo(layer, h):
        def go(r):
            halo_out[layer, pl.ds(r, ROWS), :] = dot(shalo[pl.ds(r, ROWS), :], h[...]).astype(BF)

        tiles(halos, go)

    gather_halo(0, h0)

    def halo_copy(layer, k):
        part_k = pl.ds(k * hslot, hslot)
        return pltpu.make_async_remote_copy(
            src_ref=halo_out.at[layer, part_k, :], dst_ref=halo_in.at[layer, part_k, :],
            send_sem=hs_sem.at[layer, k], recv_sem=hr_sem.at[layer, k],
            device_id=(targets[k], feat), device_id_type=MESH,
        )

    def exchange(layer, c):
        rows = pl.ds(c * ROWS, ROWS)
        return pltpu.make_async_remote_copy(
            src_ref=part.at[layer, rows, :], dst_ref=part_in.at[layer, rows, :],
            send_sem=xs_sem.at[layer, c], recv_sem=xr_sem.at[layer, c],
            device_id=(dom, peer), device_id_type=MESH,
        )

    def probe_copy(k):
        part_k = pl.ds(k * qslot, qslot)
        return pltpu.make_async_remote_copy(
            src_ref=probe_out.at[part_k, :], dst_ref=probe_in.at[part_k, :],
            send_sem=ps_sem.at[k], recv_sem=pr_sem.at[k],
            device_id=(targets[k], feat), device_id_type=MESH,
        )

    pl.semaphore_wait(barrier, 9)
    for k in range(8):
        halo_copy(0, k).start()

    def edge_selectors(r):
        select(ssrc, csrc, r)
        select(sdst, cdst, r)

    tiles(edges, edge_selectors)

    def node_selectors(r):
        here = sublanes + r
        for j in range(edges // 128):
            hit = jnp.where(here == edst[j : j + 1, :], 1.0, 0.0).astype(BF)
            tdst[pl.ds(r, ROWS), j * 128 : (j + 1) * 128] = hit

    tiles(nodes, node_selectors)

    def interp_weights(r):
        here = sublanes + r
        for j in range(probes // 128):
            lane = slice(j * 128, (j + 1) * 128)
            total = jnp.zeros((ROWS, 128), F32)
            for s in range(8):
                total = total + jnp.where(here == pslot[s : s + 1, lane], pwgt[s : s + 1, lane], 0.0)
            wint[j * 128 : (j + 1) * 128, pl.ds(r, ROWS)] = jnp.transpose(total).astype(BF)

    def edge_lat_part(layer):
        def go(r):
            rows = pl.ds(r, ROWS)
            pre[rows, :] = dot(edge[rows, :], ef[layer, 0:512, :])

        tiles(edges, go)

    def own_part(layer, h):
        def go(r):
            rows = pl.ds(r, ROWS)
            own[rows, :] = dot(ssrc[rows, 0:nodes], h[...]).astype(BF)
            there = dot(sdst[rows, :], h[...]).astype(BF)
            pre[rows, :] += dot(there, ef[layer, 1024:1536, :])

        tiles(edges, go)

    def edge_update(layer):
        def go(r):
            rows = pl.ds(r, ROWS)
            far = dot(ssrc[rows, nodes:], halo_in[layer]).astype(BF)
            hidden = pre[rows, :] + dot(own[rows, :] + far, ef[layer, 512:1024, :])
            hidden = jnp.maximum(hidden, 0.0).astype(BF)
            update = dot(hidden, es[layer])
            edge[rows, :] = (edge[rows, :].astype(F32) + layer_norm(update)).astype(BF)

        tiles(edges, go)

    def node_lat_part(layer, h):
        def go(r):
            rows = pl.ds(r, ROWS)
            hn[rows, :] = dot(h[rows, :], nf[layer, 0:512, :])

        tiles(nodes, go)

    def sum_edges(layer):
        for c in range(nodes // ROWS):
            rows = slice(c * ROWS, (c + 1) * ROWS)
            part[layer, rows, :] = dot(tdst[rows, :], edge[...]).astype(BF)
            exchange(layer, c).start()

    def node_update(layer, h, new):
        for c in range(nodes // ROWS):
            exchange(layer, c).wait()

        def go(r):
            rows = pl.ds(r, ROWS)
            summed = (part[layer, rows, :].astype(F32) + part_in[layer, rows, :].astype(F32)).astype(BF)
            hidden = hn[rows, :] + dot(summed, nf[layer, 512:1024, :])
            hidden = jnp.maximum(hidden, 0.0).astype(BF)
            update = dot(hidden, ns[layer])
            new[rows, :] = (h[rows, :].astype(F32) + layer_norm(update)).astype(BF)

        tiles(nodes, go)

    loads[1].wait()
    loads[2].wait()
    edge_lat_part(0)
    own_part(0, h0)
    loads[3].wait()
    node_lat_part(0, h0)
    loads[4].wait()
    for k in range(8):
        halo_copy(0, k).wait()
    edge_update(0)
    sum_edges(0)
    loads[6].wait()
    edge_lat_part(1)
    loads[5].wait()
    node_update(0, h0, h1)

    gather_halo(1, h1)
    for k in range(8):
        halo_copy(1, k).start()
    own_part(1, h1)
    loads[7].wait()
    node_lat_part(1, h1)
    loads[8].wait()
    for k in range(8):
        halo_copy(1, k).wait()
    edge_update(1)
    sum_edges(1)
    tiles(requests, lambda r: select(sprobe, cprobe, r))
    loads[9].wait()
    node_update(1, h1, h2)

    store = pltpu.make_async_copy(h2, out_hbm, store_sem.at[0])
    store.start()
    for c in range(4):
        rows = slice(c * 256, (c + 1) * 256)
        probe_out[rows, :] = dot(sprobe[rows, :], h2[...]).astype(BF)
        probe_copy(2 * c).start()
        probe_copy(2 * c + 1).start()
    tiles(requests, interp_weights)
    loads[10].wait()
    loads[11].wait()
    for k in range(8):
        probe_copy(k).wait()

    def decode(r):
        rows = pl.ds(r, ROWS)
        inside = (dot(wint[rows, :], probe_in[...]) + emb[rows, :].astype(F32)).astype(BF)
        hidden = jnp.maximum(dot(inside, d1[...]), 0.0).astype(BF)
        fields[:, pl.ds(r, ROWS)] = lax.dot_general(
            d2[...], hidden, (((1,), (1,)), ((), ())), preferred_element_type=F32
        )

    tiles(probes, decode)
    store.wait()


def body(
    node_lat, edge_lat, edge_src, edge_dst, halo_rows, probe_rows, probe_slot, probe_wgt, probe_embed,
    edge_first, edge_second, node_first, node_second, decode_first, decode_second,
):
    nodes, width = node_lat.shape
    edges, probes = edge_lat.shape[0], probe_embed.shape[0]
    halos, requests = halo_rows.size, probe_rows.size
    layers, fields = edge_first.shape[0], decode_second.shape[0]
    anywhere = pl.BlockSpec(memory_space=pl.ANY)
    vmem = pl.BlockSpec(memory_space=pltpu.VMEM)
    dma = pltpu.SemaphoreType.DMA
    return pl.pallas_call(
        kernel,
        out_shape=(
            jax.ShapeDtypeStruct((nodes, width), BF),
            jax.ShapeDtypeStruct((fields, probes), F32),
        ),
        in_specs=[anywhere] * 2 + [vmem] * 6 + [anywhere] * 6 + [vmem],
        out_specs=(anywhere, vmem),
        scratch_shapes=[
            pltpu.VMEM((nodes, width), BF), pltpu.VMEM((nodes, width), BF), pltpu.VMEM((nodes, width), BF),
            pltpu.VMEM((edges, width), BF), pltpu.VMEM((probes, width), BF),
            pltpu.VMEM(edge_first.shape, BF), pltpu.VMEM(edge_second.shape, BF),
            pltpu.VMEM(node_first.shape, BF), pltpu.VMEM(node_second.shape, BF), pltpu.VMEM(decode_first.shape, BF),
            pltpu.VMEM((edges, 128), jnp.int32), pltpu.VMEM((edges, 128), jnp.int32),
            pltpu.VMEM((halos, 128), jnp.int32), pltpu.VMEM((requests, 128), jnp.int32),
            pltpu.VMEM((edges, nodes + halos), BF), pltpu.VMEM((edges, nodes), BF), pltpu.VMEM((nodes, edges), BF),
            pltpu.VMEM((halos, nodes), BF), pltpu.VMEM((requests, nodes), BF), pltpu.VMEM((probes, requests), BF),
            pltpu.VMEM((edges, width), BF), pltpu.VMEM((edges, width), F32), pltpu.VMEM((nodes, width), F32),
            pltpu.VMEM((layers, nodes, width), BF), pltpu.VMEM((layers, nodes, width), BF),
            pltpu.VMEM((layers, halos, width), BF), pltpu.VMEM((layers, halos, width), BF),
            pltpu.VMEM((requests, width), BF), pltpu.VMEM((requests, width), BF),
            dma((12,)), dma((1,)), dma((layers, 8)), dma((layers, 8)), dma((layers, 4)), dma((layers, 4)),
            dma((8,)), dma((8,)),
        ],
        compiler_params=pltpu.CompilerParams(
            collective_id=0, has_side_effects=True, vmem_limit_bytes=56 * 1024 * 1024
        ),
    )(
        node_lat, edge_lat, edge_src.reshape(-1, 128), edge_dst.reshape(-1, 128), halo_rows, probe_rows,
        probe_slot.T, probe_wgt.T, probe_embed,
        edge_first, edge_second, node_first, node_second, decode_first, decode_second,
    )


def solution(mesh):
    both = P(("dom", "feat"), None)
    return jax.shard_map(
        body,
        mesh=mesh,
        in_specs=(
            P("dom", None), both, P(("dom", "feat")), P(("dom", "feat")), P("dom", None),
            both, both, both, both, P(), P(), P(), P(), P(), P(),
        ),
        out_specs=(P("dom", None), P(None, ("dom", "feat"))),
        check_vma=False,
    )
```

profile of v0, /device:TPU:1, one launch (start us, length us, event | category | flops | bytes accessed | tf_op | source)
XLA Modules:
  0.0 75.9 jit_solution(16357044213919043755)
XLA Ops:
  0.6 71.7 %shard_map.158 = (bf16[1024,512]{1,0:T(8,128)(2,1)}, f32[4,512]{1,0:T(4,128)}) custom-call(bf16[1024,512]{1,0:T(8,128)(2,1)} %node_hbm.1, bf16[1024,512]{1,0:T(8,128)(2,1)} %edge_hbm.1, s32[8,128]{1,0:T(8,128)} %bitcast.6, s32[8,128]{1,0:T(8,128)} %bitcast.7, s32[8,64]{1,0:T(8,128)} %hrows.1, s32[8,128]{1,0:T(8,128)} %prows.1, s32[8,512]{1,0:T(8,128)} %bitcast.4, ...), custom_call_target="tpu_custom_call" | custom-call | tf_op jit(solution)/shard_map/pallas_call | solution.py:274
  72.3 2.3 %copy.19 = bf16[1024,512]{1,0:T(8,128)(2,1)} copy(bf16[1024,512]{1,0:T(8,128)(2,1)} %get-tuple-element.4) | data formatting | bytes 2097152
  74.6 1.3 %copy.20 = f32[4,512]{1,0:T(4,128)} copy(f32[4,512]{1,0:T(4,128)} %get-tuple-element.5) | data formatting | bytes 16384
where the time goes:
time: 76.5 us; the launch traced here: 75.9 us
  Pallas kernels  71.7 us (94%)
  local copies, waits for them, and re-layouts  3.56 us (5%)
    pallas_call x1, Pallas kernels, body(): pl.pallas_call(kernel, out_shape=(jax.ShapeDtypeStruct((nodes, width), BF...  71.7 us
    unnamed x2, local copies, waits for them, and re-layouts  3.56 us

commit v1 on v0

v1 whole, which is shorter than its diff:
```python
import jax
import jax.numpy as jnp
from jax import lax
from jax.experimental import pallas as pl
from jax.experimental.pallas import tpu as pltpu
from jax.sharding import PartitionSpec as P

SPAN = 4
BF = jnp.bfloat16
F32 = jnp.float32
MESH = pl.DeviceIdType.MESH
OFFSETS = (1, -1, SPAN, -SPAN, SPAN + 1, -SPAN - 1, SPAN - 1, 1 - SPAN)
ROWS = 512
SEL = 256
FAR_FIRST = (2, 3, 0, 1)


def dot(a, b):
    return jnp.dot(a, b, preferred_element_type=F32)


def layer_norm(values):
    centre = jnp.mean(values, axis=-1, keepdims=True)
    shifted = values - centre
    spread = jnp.mean(shifted * shifted, axis=-1, keepdims=True)
    return shifted * lax.rsqrt(spread + 1e-05)


def looped(count, body):
    def step(i, carry):
        body(pl.multiple_of(i * SEL, SEL))
        return carry

    lax.fori_loop(0, count // SEL, step, 0)


def unrolled(count, body):
    for r in range(0, count, ROWS):
        body(slice(r, r + ROWS))


def column(row):
    return jnp.transpose(jnp.broadcast_to(row, (128, 128)))


def kernel(
    node_hbm, edge_hbm, esrc, edst, hrows, prows, pslot, pwgt, emb_hbm,
    ef_hbm, es_hbm, nf_hbm, ns_hbm, d1_hbm, d2,
    out_hbm, fields,
    h0, h1, h2, edge, emb, ef, es, nf, ns, d1,
    csrc, cdst, chalo, cprobe, prows_in, ssrc, sdst, tdst, shalo, thalo, sprobe, tprobe, wint,
    own, pre, hn, hnh, hnp, part, part_in, halo_part, halo_part_in, halo_out, halo_in,
    pick, mine, theirs, theirs_in, probe_out, probe_in,
    load_sem, store_sem, hs_sem, hr_sem, xs_sem, xr_sem, ys_sem, yr_sem, zs_sem, zr_sem, ps_sem, pr_sem, is_sem, ir_sem,
):
    nodes, edges = h0.shape[0], edge.shape[0]
    halos, requests, probes = halo_in.shape[1], probe_in.shape[0], emb.shape[0]
    hslot, qslot = halos // 8, requests // 8
    count = lax.axis_size("dom")
    dom, feat = lax.axis_index("dom"), lax.axis_index("feat")
    peer = 1 - feat
    targets = [lax.rem(dom + off + count, count) for off in OFFSETS]

    barrier = pltpu.get_barrier_semaphore()
    for target in targets:
        pl.semaphore_signal(barrier, inc=1, device_id=(target, feat), device_id_type=MESH)
    pl.semaphore_signal(barrier, inc=1, device_id=(dom, peer), device_id_type=MESH)

    pairs = [
        (node_hbm, h0), (edge_hbm, edge),
        (ef_hbm.at[0], ef.at[0]), (nf_hbm.at[0], nf.at[0]), (es_hbm.at[0], es.at[0]), (ns_hbm.at[0], ns.at[0]),
        (ef_hbm.at[1], ef.at[1]), (nf_hbm.at[1], nf.at[1]), (es_hbm.at[1], es.at[1]), (ns_hbm.at[1], ns.at[1]),
        (emb_hbm, emb), (d1_hbm, d1),
    ]
    loads = [pltpu.make_async_copy(src, dst, load_sem.at[i]) for i, (src, dst) in enumerate(pairs)]
    for load in loads:
        load.start()

    def remote(src, dst, send, recv, device):
        return pltpu.make_async_remote_copy(
            src_ref=src, dst_ref=dst, send_sem=send, recv_sem=recv, device_id=device, device_id_type=MESH
        )

    def halo_copy(layer, k):
        rows = pl.ds(k * hslot, hslot)
        return remote(halo_out.at[layer, rows, :], halo_in.at[layer, rows, :],
                      hs_sem.at[layer, k], hr_sem.at[layer, k], (targets[k], feat))

    def exchange(layer, c):
        rows = pl.ds(c * ROWS, ROWS)
        return remote(part.at[layer, rows, :], part_in.at[layer, rows, :],
                      xs_sem.at[layer, c], xr_sem.at[layer, c], (dom, peer))

    def halo_exchange(c):
        rows = pl.ds(c * SEL, SEL)
        return remote(halo_part.at[rows, :], halo_part_in.at[rows, :], ys_sem.at[c], yr_sem.at[c], (dom, peer))

    def probe_exchange(c):
        rows = pl.ds(c * 2 * qslot, 2 * qslot)
        return remote(theirs.at[rows, :], theirs_in.at[rows, :], zs_sem.at[c], zr_sem.at[c], (dom, peer))

    def probe_copy(k):
        rows = pl.ds(k * qslot, qslot)
        return remote(probe_out.at[rows, :], probe_in.at[rows, :], ps_sem.at[k], pr_sem.at[k], (targets[k], feat))

    index_copy = remote(prows, prows_in, is_sem.at[0], ir_sem.at[0], (dom, peer))

    lanes = lax.broadcasted_iota(jnp.int32, (SEL, 128), 1)
    sublanes = lax.broadcasted_iota(jnp.int32, (SEL, 128), 0)

    def select(out, col, r):
        here = col[pl.ds(r, SEL), :]
        for j in range(out.shape[1] // 128):
            hit = jnp.where(here == lanes + j * 128, 1.0, 0.0).astype(BF)
            out[pl.ds(r, SEL), j * 128 : (j + 1) * 128] = hit

    def incident(out, here, r):
        for j in range(edges // 128):
            hit = jnp.where(here == edst[j : j + 1, :], 1.0, 0.0).astype(BF)
            out[pl.ds(r, SEL), j * 128 : (j + 1) * 128] = hit

    for j in range(halos // 128):
        pair = jnp.concatenate([hrows[2 * j : 2 * j + 1, :], hrows[2 * j + 1 : 2 * j + 2, :]], axis=1)
        chalo[j * 128 : (j + 1) * 128, :] = column(pair)
    looped(halos, lambda r: select(shalo, chalo, r))
    loads[0].wait()
    halo_out[0] = dot(shalo[...], h0[...]).astype(BF)
    pl.semaphore_wait(barrier, 9)
    for k in range(7, -1, -1):
        halo_copy(0, k).start()
    index_copy.start()

    for j in range(edges // 128):
        csrc[j * 128 : (j + 1) * 128, :] = column(esrc[j : j + 1, :])
        cdst[j * 128 : (j + 1) * 128, :] = column(edst[j : j + 1, :])
    looped(edges, lambda r: (select(ssrc, csrc, r), select(sdst, cdst, r), None)[2])

    def edge_lat_part(layer):
        def go(rows):
            pre[rows, :] = dot(edge[rows, :], ef[layer, 0:512, :])

        unrolled(edges, go)

    def own_part(layer, h):
        def go(rows):
            own[rows, :] = dot(ssrc[rows, 0:nodes], h[...]).astype(BF)
            there = dot(sdst[rows, :], h[...]).astype(BF)
            pre[rows, :] += dot(there, ef[layer, 1024:1536, :])

        unrolled(edges, go)

    def edge_update(layer):
        def go(rows):
            far = dot(ssrc[rows, nodes:], halo_in[layer]).astype(BF)
            hidden = pre[rows, :] + dot(own[rows, :] + far, ef[layer, 512:1024, :])
            hidden = jnp.maximum(hidden, 0.0).astype(BF)
            update = dot(hidden, es[layer])
            edge[rows, :] = (edge[rows, :].astype(F32) + layer_norm(update)).astype(BF)

        unrolled(edges, go)

    def node_lat_part(layer, h):
        def go(rows):
            hn[rows, :] = dot(h[rows, :], nf[layer, 0:512, :])

        unrolled(nodes, go)

    def mlp(layer, start, first, one, other):
        summed = (one.astype(F32) + other.astype(F32)).astype(BF)
        hidden = jnp.maximum(first + dot(summed, nf[layer, 512:1024, :]), 0.0).astype(BF)
        return (start.astype(F32) + layer_norm(dot(hidden, ns[layer]))).astype(BF)

    def sum_edges(layer, c):
        rows = slice(c * ROWS, (c + 1) * ROWS)
        part[layer, rows, :] = dot(tdst[rows, :], edge[...]).astype(BF)
        exchange(layer, c).start()

    def node_update(layer, h, new):
        for c in range(nodes // ROWS):
            rows = slice(c * ROWS, (c + 1) * ROWS)
            exchange(layer, c).wait_recv()
            new[rows, :] = mlp(layer, h[rows, :], hn[rows, :], part[layer, rows, :], part_in[layer, rows, :])

    loads[1].wait()
    loads[2].wait()
    edge_lat_part(0)
    own_part(0, h0)
    loads[3].wait()
    node_lat_part(0, h0)
    hnh[...] = dot(halo_out[0], nf[0, 0:512, :])
    looped(halos, lambda r: incident(thalo, chalo[pl.ds(r, SEL), :], r))
    looped(nodes, lambda r: incident(tdst, sublanes + r, r))
    index_copy.wait_recv()
    for j in range(requests // 128):
        cprobe[2 * j * 128 : (2 * j + 1) * 128, :] = column(prows_in[j : j + 1, :])
        cprobe[(2 * j + 1) * 128 : (2 * j + 2) * 128, :] = column(prows[j : j + 1, :])
    looped(2 * requests, lambda r: incident(tprobe, cprobe[pl.ds(r, SEL), :], r))
    loads[4].wait()
    loads[5].wait()
    for k in range(8):
        halo_copy(0, k).wait_recv()
    edge_update(0)

    for c in (1, 0):
        rows = slice(c * SEL, (c + 1) * SEL)
        halo_part[rows, :] = dot(thalo[rows, :], edge[...]).astype(BF)
        halo_exchange(c).start()
    sum_edges(0, 0)
    for c in (1, 0):
        rows = slice(c * SEL, (c + 1) * SEL)
        halo_exchange(c).wait_recv()
        halo_out[1, rows, :] = mlp(0, halo_out[0, rows, :], hnh[rows, :], halo_part[rows, :], halo_part_in[rows, :])
        for k in range(4 * c, 4 * c + 4):
            halo_copy(1, k).start()
    sum_edges(0, 1)
    for load in loads[6:]:
        load.wait()
    edge_lat_part(1)
    node_update(0, h0, h1)

    own_part(1, h1)

    def pick_rows(r):
        here = cprobe[pl.ds(2 * r + 128, 128), :]
        for half in range(2):
            here = cprobe[pl.ds(2 * r + 256 * half + 128, 128), :]
            for j in range(nodes // 128):
                hit = jnp.where(here == lanes[0:128] + j * 128, 1.0, 0.0).astype(BF)
                sprobe[pl.ds(r + 128 * half, 128), j * 128 : (j + 1) * 128] = hit

    looped(requests, pick_rows)

    def pick_part(rows):
        picked = dot(sprobe[rows, :], h1[...]).astype(BF)
        pick[rows, :] = picked
        hnp[rows, :] = dot(picked, nf[1, 0:512, :])

    unrolled(requests, pick_part)
    for k in range(8):
        halo_copy(1, k).wait_recv()
    edge_update(1)

    def probe_sums(c):
        here = 4 * qslot * c
        both = dot(tprobe[here : here + 4 * qslot, :], edge[...]).astype(BF)
        for i in range(2):
            rows = slice((2 * c + i) * qslot, (2 * c + i + 1) * qslot)
            theirs[rows, :] = both[2 * i * qslot : (2 * i + 1) * qslot]
            mine[rows, :] = both[(2 * i + 1) * qslot : (2 * i + 2) * qslot]
        probe_exchange(c).start()

    def probe_rows(c):
        rows = slice(2 * c * qslot, (2 * c + 2) * qslot)
        probe_exchange(c).wait_recv()
        probe_out[rows, :] = mlp(1, pick[rows, :], hnp[rows, :], mine[rows, :], theirs_in[rows, :])
        probe_copy(2 * c).start()
        probe_copy(2 * c + 1).start()

    probe_sums(FAR_FIRST[0])
    probe_sums(FAR_FIRST[1])
    probe_rows(FAR_FIRST[0])
    probe_sums(FAR_FIRST[2])
    probe_rows(FAR_FIRST[1])
    probe_sums(FAR_FIRST[3])
    probe_rows(FAR_FIRST[2])
    probe_rows(FAR_FIRST[3])

    sum_edges(1, 0)
    sum_edges(1, 1)
    node_lat_part(1, h1)

    def interp_weights(r):
        here = sublanes + r
        for j in range(probes // 128):
            lane = slice(j * 128, (j + 1) * 128)
            total = jnp.zeros((SEL, 128), F32)
            for s in range(8):
                total = total + jnp.where(here == pslot[s : s + 1, lane], pwgt[s : s + 1, lane], 0.0)
            wint[j * 128 : (j + 1) * 128, pl.ds(r, SEL)] = jnp.transpose(total).astype(BF)

    looped(requests, interp_weights)
    node_update(1, h1, h2)
    store = pltpu.make_async_copy(h2, out_hbm, store_sem.at[0])
    store.start()

    total = emb[...].astype(F32)
    for c in FAR_FIRST:
        rows = slice(2 * c * qslot, (2 * c + 2) * qslot)
        probe_copy(2 * c).wait_recv()
        probe_copy(2 * c + 1).wait_recv()
        total = total + dot(wint[:, rows], probe_in[rows, :])
    hidden = jnp.maximum(dot(total.astype(BF), d1[...]), 0.0).astype(BF)
    fields[...] = lax.dot_general(d2[...], hidden, (((1,), (1,)), ((), ())), preferred_element_type=F32)

    store.wait()
    index_copy.wait_send()
    for k in range(8):
        halo_copy(0, k).wait_send()
        halo_copy(1, k).wait_send()
        probe_copy(k).wait_send()
    for c in range(2):
        exchange(0, c).wait_send()
        exchange(1, c).wait_send()
        halo_exchange(c).wait_send()
    for c in range(4):
        probe_exchange(c).wait_send()


def handover(surface, fields, surface_out, fields_out, rows, line, in_sem, out_sem):
    part = surface.shape[0] // 4
    pieces = [(fields, line, fields_out)]
    for i in range(4):
        cut = pl.ds(i * part, part)
        pieces.append((surface.at[cut, :], rows.at[cut, :], surface_out.at[cut, :]))
    ins = [pltpu.make_async_copy(src, mid, in_sem.at[i]) for i, (src, mid, _) in enumerate(pieces)]
    outs = [pltpu.make_async_copy(mid, dst, out_sem.at[i]) for i, (_, mid, dst) in enumerate(pieces)]
    for move in ins:
        move.start()
    for move, onward in zip(ins, outs):
        move.wait()
        onward.start()
    for onward in outs:
        onward.wait()


def body(
    node_lat, edge_lat, edge_src, edge_dst, halo_rows, probe_rows, probe_slot, probe_wgt, probe_embed,
    edge_first, edge_second, node_first, node_second, decode_first, decode_second,
):
    nodes, width = node_lat.shape
    edges, probes = edge_lat.shape[0], probe_embed.shape[0]
    halos, requests = halo_rows.size, probe_rows.size
    layers, fields = edge_first.shape[0], decode_second.shape[0]
    anywhere = pl.BlockSpec(memory_space=pl.ANY)
    vmem = pl.BlockSpec(memory_space=pltpu.VMEM)
    dma = pltpu.SemaphoreType.DMA
    outs = (
        jax.ShapeDtypeStruct((nodes, width), BF),
        jax.ShapeDtypeStruct((fields, probes), F32),
    )

    def buf(*shape, dtype=BF):
        return pltpu.VMEM(shape, dtype)

    i32 = jnp.int32
    made = pl.pallas_call(
        kernel,
        out_shape=outs,
        in_specs=[anywhere] * 2 + [vmem] * 6 + [anywhere] * 6 + [vmem],
        out_specs=(anywhere, vmem),
        scratch_shapes=[
            buf(nodes, width), buf(nodes, width), buf(nodes, width), buf(edges, width), buf(probes, width),
            buf(*edge_first.shape), buf(*edge_second.shape), buf(*node_first.shape), buf(*node_second.shape),
            buf(*decode_first.shape),
            buf(edges, 128, dtype=i32), buf(edges, 128, dtype=i32), buf(halos, 128, dtype=i32),
            buf(2 * requests, 128, dtype=i32), buf(*probe_rows.shape, dtype=i32),
            buf(edges, nodes + halos), buf(edges, nodes), buf(nodes, edges), buf(halos, nodes), buf(halos, edges),
            buf(requests, nodes), buf(2 * requests, edges), buf(probes, requests),
            buf(edges, width), buf(edges, width, dtype=F32), buf(nodes, width, dtype=F32),
            buf(halos, width, dtype=F32), buf(requests, width, dtype=F32),
            buf(layers, nodes, width), buf(layers, nodes, width), buf(halos, width), buf(halos, width),
            buf(layers, halos, width), buf(layers, halos, width),
            buf(requests, width), buf(requests, width), buf(requests, width), buf(requests, width),
            buf(requests, width), buf(requests, width),
            dma((12,)), dma((1,)), dma((layers, 8)), dma((layers, 8)), dma((layers, 2)), dma((layers, 2)),
            dma((2,)), dma((2,)), dma((4,)), dma((4,)), dma((8,)), dma((8,)), dma((1,)), dma((1,)),
        ],
        compiler_params=pltpu.CompilerParams(
            collective_id=0, has_side_effects=True, vmem_limit_bytes=60 * 1024 * 1024
        ),
    )(
        node_lat, edge_lat, edge_src.reshape(-1, 128), edge_dst.reshape(-1, 128), halo_rows, probe_rows,
        probe_slot.T, probe_wgt.T, probe_embed,
        edge_first, edge_second, node_first, node_second, decode_first, decode_second,
    )
    return pl.pallas_call(
        handover,
        out_shape=outs,
        in_specs=[anywhere] * 2,
        out_specs=(anywhere, anywhere),
        scratch_shapes=[buf(nodes, width), buf(fields, probes, dtype=F32), dma((5,)), dma((5,))],
    )(*made)


def solution(mesh):
    both = P(("dom", "feat"), None)
    return jax.shard_map(
        body,
        mesh=mesh,
        in_specs=(
            P("dom", None), both, P(("dom", "feat")), P(("dom", "feat")), P("dom", None),
            both, both, both, both, P(), P(), P(), P(), P(), P(),
        ),
        out_specs=(P("dom", None), P(None, ("dom", "feat"))),
        check_vma=False,
    )
```

time: 76.5 us -> 62.6 us (0.82)
  Pallas kernels: 71.7 us -> 61.6 us
  local copies, waits for them, and re-layouts: 3.56 us -> 0 us
    pallas_call x1 -> x2, Pallas kernels: 71.7 us -> 61.6 us  [the longest x1 59.6 us: body(): pl.pallas_call(kernel, out_shape=outs, in_specs=[anywhere] * 2 + [vmem] *...]
    unnamed x2 -> x0, local copies, waits for them, and re-layouts: 3.56 us -> none
where the time goes in v1:
time: 62.6 us; the launch traced here: 62.4 us
  Pallas kernels  61.6 us (98%)
  between operations  0.8 us (1%)
    pallas_call x1, Pallas kernels, body(): pl.pallas_call(kernel, out_shape=outs, in_specs=[anywhere] * 2 + [vmem] *...  59.6 us
    pallas_call x1, Pallas kernels, body(): pl.pallas_call(handover, out_shape=outs, in_specs=[anywhere] * 2, out_spe...  2.01 us

profile of v1, /device:TPU:1, one launch (start us, length us, event | category | flops | bytes accessed | tf_op | source)
XLA Modules:
  0.0 62.4 jit_solution(5942302442066961087)
XLA Ops:
  0.6 59.6 %shard_map.158 = (bf16[1024,512]{1,0:T(8,128)(2,1)}, f32[4,512]{1,0:T(4,128)}) custom-call(bf16[1024,512]{1,0:T(8,128)(2,1)} %node_hbm.1, bf16[1024,512]{1,0:T(8,128)(2,1)} %edge_hbm.1, s32[8,128]{1,0:T(8,128)} %bitcast.6, s32[8,128]{1,0:T(8,128)} %bitcast.7, s32[8,64]{1,0:T(8,128)} %hrows.1, s32[8,128]{1,0:T(8,128)} %prows.1, s32[8,512]{1,0:T(8,128)} %bitcast.4, ...), custom_call_target="tpu_custom_call" | custom-call | tf_op jit(solution)/shard_map/pallas_call | solution.py:346
  60.3 2.0 %shard_map.159 = (bf16[1024,512]{1,0:T(8,128)(2,1)}, f32[4,512]{1,0:T(4,128)}) custom-call(bf16[1024,512]{1,0:T(8,128)(2,1)} %get-tuple-element.4.surface, f32[4,512]{1,0:T(4,128)} %get-tuple-element.5.fields), custom_call_target="tpu_custom_call" | custom-call | tf_op jit(solution)/shard_map/pallas_call | solution.py:376

commit v2 on v1

--- a/solution.py
+++ b/solution.py
@@ -44,56 +44,66 @@
 
 
 def kernel(
-    node_hbm, edge_hbm, esrc, edst, hrows, prows, pslot, pwgt, emb_hbm,
-    ef_hbm, es_hbm, nf_hbm, ns_hbm, d1_hbm, d2,
+    node_hbm, edge_hbm, esrc_hbm, edst_hbm, hrows_hbm, prows_hbm, pslot_hbm, pwgt_hbm, emb_hbm,
+    ef_hbm, es_hbm, nf_hbm, ns_hbm, d1_hbm, d2_hbm,
     out_hbm, fields,
-    h0, h1, h2, edge, emb, ef, es, nf, ns, d1,
+    esrc, edst, hrows, prows, pslot, pwgt, d2, h0, h1, h2, edge, emb, ef, es, nf, ns, d1,
     csrc, cdst, chalo, cprobe, prows_in, ssrc, sdst, tdst, shalo, thalo, sprobe, tprobe, wint,
-    own, pre, hn, hnh, hnp, part, part_in, halo_part, halo_part_in, halo_out, halo_in,
-    pick, mine, theirs, theirs_in, probe_out, probe_in,
+    own, pre, hn, hnh, hnp, part, part_in, halo_mine, halo_theirs, halo_theirs_in, halo_out, halo_in,
+    pick, mine, theirs, theirs_in, probe_out, probe_in, relay_in,
     load_sem, store_sem, hs_sem, hr_sem, xs_sem, xr_sem, ys_sem, yr_sem, zs_sem, zr_sem, ps_sem, pr_sem, is_sem, ir_sem,
+    fs_sem, fr_sem, rs_sem, rr_sem, gs_sem,
 ):
     nodes, edges = h0.shape[0], edge.shape[0]
     halos, requests, probes = halo_in.shape[1], probe_in.shape[0], emb.shape[0]
-    hslot, qslot = halos // 8, requests // 8
+    half, hslot, qslot = halos // 2, halos // 16, requests // 8
     count = lax.axis_size("dom")
     dom, feat = lax.axis_index("dom"), lax.axis_index("feat")
     peer = 1 - feat
     targets = [lax.rem(dom + off + count, count) for off in OFFSETS]
 
+    place = lax.rem(dom, SPAN)
+    is_first, is_last = place == 0, place == SPAN - 1
+
+    pairs = [
+        (hrows_hbm, hrows), (node_hbm, h0),
+        (esrc_hbm, esrc), (edst_hbm, edst), (edge_hbm, edge),
+        (ef_hbm.at[0], ef.at[0]), (nf_hbm.at[0], nf.at[0]), (prows_hbm, prows),
+        (es_hbm.at[0], es.at[0]), (ns_hbm.at[0], ns.at[0]),
+        (ef_hbm.at[1], ef.at[1]), (nf_hbm.at[1], nf.at[1]), (es_hbm.at[1], es.at[1]), (ns_hbm.at[1], ns.at[1]),
+        (pslot_hbm, pslot), (pwgt_hbm, pwgt), (emb_hbm, emb), (d1_hbm, d1), (d2_hbm, d2),
+    ]
+    loads = [pltpu.make_async_copy(src, dst, load_sem.at[i]) for i, (src, dst) in enumerate(pairs)]
+    loads[0].start()
+    loads[1].start()
+
     barrier = pltpu.get_barrier_semaphore()
     for target in targets:
         pl.semaphore_signal(barrier, inc=1, device_id=(target, feat), device_id_type=MESH)
     pl.semaphore_signal(barrier, inc=1, device_id=(dom, peer), device_id_type=MESH)
 
-    pairs = [
-        (node_hbm, h0), (edge_hbm, edge),
-        (ef_hbm.at[0], ef.at[0]), (nf_hbm.at[0], nf.at[0]), (es_hbm.at[0], es.at[0]), (ns_hbm.at[0], ns.at[0]),
-        (ef_hbm.at[1], ef.at[1]), (nf_hbm.at[1], nf.at[1]), (es_hbm.at[1], es.at[1]), (ns_hbm.at[1], ns.at[1]),
-        (emb_hbm, emb), (d1_hbm, d1),
-    ]
-    loads = [pltpu.make_async_copy(src, dst, load_sem.at[i]) for i, (src, dst) in enumerate(pairs)]
-    for load in loads:
-        load.start()
-
     def remote(src, dst, send, recv, device):
         return pltpu.make_async_remote_copy(
             src_ref=src, dst_ref=dst, send_sem=send, recv_sem=recv, device_id=device, device_id_type=MESH
         )
 
     def halo_copy(layer, k):
-        rows = pl.ds(k * hslot, hslot)
-        return remote(halo_out.at[layer, rows, :], halo_in.at[layer, rows, :],
+        here = pl.ds(k * hslot, hslot)
+        there = pl.ds(pl.multiple_of(feat * half + k * hslot, hslot), hslot)
+        return remote(halo_out.at[layer, here, :], halo_in.at[layer, there, :],
                       hs_sem.at[layer, k], hr_sem.at[layer, k], (targets[k], feat))
+
+    def halo_share(layer, c):
+        rows = pl.ds(pl.multiple_of(feat * half + c * 4 * hslot, 4 * hslot), 4 * hslot)
+        return remote(halo_in.at[layer, rows, :], halo_in.at[layer, rows, :],
+                      fs_sem.at[layer, c], fr_sem.at[layer, c], (dom, peer))
 
     def exchange(layer, c):
         rows = pl.ds(c * ROWS, ROWS)
         return remote(part.at[layer, rows, :], part_in.at[layer, rows, :],
                       xs_sem.at[layer, c], xr_sem.at[layer, c], (dom, peer))
 
-    def halo_exchange(c):
-        rows = pl.ds(c * SEL, SEL)
-        return remote(halo_part.at[rows, :], halo_part_in.at[rows, :], ys_sem.at[c], yr_sem.at[c], (dom, peer))
+    halo_exchange = remote(halo_theirs, halo_theirs_in, ys_sem.at[0], yr_sem.at[0], (dom, peer))
 
     def probe_exchange(c):
         rows = pl.ds(c * 2 * qslot, 2 * qslot)
@@ -102,6 +112,16 @@
     def probe_copy(k):
         rows = pl.ds(k * qslot, qslot)
         return remote(probe_out.at[rows, :], probe_in.at[rows, :], ps_sem.at[k], pr_sem.at[k], (targets[k], feat))
+
+    def relay_out(k):
+        rows = pl.ds(k * qslot, qslot)
+        return remote(probe_out.at[rows, :], relay_in, rs_sem.at[0], rr_sem.at[0], (targets[k - 4], feat))
+
+    def relay_on(k):
+        rows = pl.ds(k * qslot, qslot)
+        return remote(relay_in, probe_in.at[rows, :], gs_sem.at[0], pr_sem.at[k], (targets[k - 2], feat))
+
+    relays = ((4, is_last, is_first), (5, is_first, is_last))
 
     index_copy = remote(prows, prows_in, is_sem.at[0], ir_sem.at[0], (dom, peer))
 
@@ -119,19 +139,29 @@
             hit = jnp.where(here == edst[j : j + 1, :], 1.0, 0.0).astype(BF)
             out[pl.ds(r, SEL), j * 128 : (j + 1) * 128] = hit
 
-    for j in range(halos // 128):
-        pair = jnp.concatenate([hrows[2 * j : 2 * j + 1, :], hrows[2 * j + 1 : 2 * j + 2, :]], axis=1)
-        chalo[j * 128 : (j + 1) * 128, :] = column(pair)
-    looped(halos, lambda r: select(shalo, chalo, r))
     loads[0].wait()
+    for g, core in enumerate((feat, peer)):
+        chosen = hrows[:, 0:hslot] + (hrows[:, hslot : 2 * hslot] - hrows[:, 0:hslot]) * core
+        for j in range(half // 128):
+            row = jnp.concatenate([chosen[k : k + 1, :] for k in range(4 * j, 4 * j + 4)], axis=1)
+            chalo[g * half + j * 128 : g * half + (j + 1) * 128, :] = column(row)
+    looped(half, lambda r: select(shalo, chalo, r))
+    loads[1].wait()
+    for load in loads[2:]:
+        load.start()
     halo_out[0] = dot(shalo[...], h0[...]).astype(BF)
     pl.semaphore_wait(barrier, 9)
     for k in range(7, -1, -1):
         halo_copy(0, k).start()
-    index_copy.start()
-
+
+    loads[2].wait()
+    loads[3].wait()
+    bits = hslot.bit_length() - 1
     for j in range(edges // 128):
-        csrc[j * 128 : (j + 1) * 128, :] = column(esrc[j : j + 1, :])
+        sender = esrc[j : j + 1, :]
+        far = sender - nodes
+        far = ((far >> bits) & 1) * half + (far >> (bits + 1)) * hslot + (far & (hslot - 1))
+        csrc[j * 128 : (j + 1) * 128, :] = column(jnp.where(sender < nodes, sender, far + nodes))
         cdst[j * 128 : (j + 1) * 128, :] = column(edst[j : j + 1, :])
     looped(edges, lambda r: (select(ssrc, csrc, r), select(sdst, cdst, r), None)[2])
 
@@ -181,52 +211,58 @@
             exchange(layer, c).wait_recv()
             new[rows, :] = mlp(layer, h[rows, :], hn[rows, :], part[layer, rows, :], part_in[layer, rows, :])
 
-    loads[1].wait()
-    loads[2].wait()
+    def share_halo(layer):
+        for c in range(2):
+            for k in range(4 * c, 4 * c + 4):
+                halo_copy(layer, k).wait_recv()
+            halo_share(layer, c).start()
+
+    loads[4].wait()
+    loads[5].wait()
     edge_lat_part(0)
     own_part(0, h0)
-    loads[3].wait()
+    loads[6].wait()
     node_lat_part(0, h0)
     hnh[...] = dot(halo_out[0], nf[0, 0:512, :])
     looped(halos, lambda r: incident(thalo, chalo[pl.ds(r, SEL), :], r))
     looped(nodes, lambda r: incident(tdst, sublanes + r, r))
+    loads[7].wait()
+    index_copy.start()
+    share_halo(0)
     index_copy.wait_recv()
     for j in range(requests // 128):
         cprobe[2 * j * 128 : (2 * j + 1) * 128, :] = column(prows_in[j : j + 1, :])
         cprobe[(2 * j + 1) * 128 : (2 * j + 2) * 128, :] = column(prows[j : j + 1, :])
     looped(2 * requests, lambda r: incident(tprobe, cprobe[pl.ds(r, SEL), :], r))
-    loads[4].wait()
-    loads[5].wait()
-    for k in range(8):
-        halo_copy(0, k).wait_recv()
+    loads[8].wait()
+    loads[9].wait()
+    for c in range(2):
+        halo_share(0, c).wait_recv()
     edge_update(0)
 
-    for c in (1, 0):
-        rows = slice(c * SEL, (c + 1) * SEL)
-        halo_part[rows, :] = dot(thalo[rows, :], edge[...]).astype(BF)
-        halo_exchange(c).start()
+    halo_theirs[...] = dot(thalo[half:, :], edge[...]).astype(BF)
+    halo_exchange.start()
+    halo_mine[...] = dot(thalo[0:half, :], edge[...]).astype(BF)
     sum_edges(0, 0)
-    for c in (1, 0):
-        rows = slice(c * SEL, (c + 1) * SEL)
-        halo_exchange(c).wait_recv()
-        halo_out[1, rows, :] = mlp(0, halo_out[0, rows, :], hnh[rows, :], halo_part[rows, :], halo_part_in[rows, :])
-        for k in range(4 * c, 4 * c + 4):
-            halo_copy(1, k).start()
+    halo_exchange.wait_recv()
+    halo_out[1] = mlp(0, halo_out[0], hnh[...], halo_mine[...], halo_theirs_in[...])
+    for k in range(7, -1, -1):
+        halo_copy(1, k).start()
     sum_edges(0, 1)
-    for load in loads[6:]:
+    for load in loads[10:]:
         load.wait()
     edge_lat_part(1)
     node_update(0, h0, h1)
 
     own_part(1, h1)
+    share_halo(1)
 
     def pick_rows(r):
-        here = cprobe[pl.ds(2 * r + 128, 128), :]
-        for half in range(2):
-            here = cprobe[pl.ds(2 * r + 256 * half + 128, 128), :]
+        for side in range(2):
+            here = cprobe[pl.ds(2 * r + 256 * side + 128, 128), :]
             for j in range(nodes // 128):
                 hit = jnp.where(here == lanes[0:128] + j * 128, 1.0, 0.0).astype(BF)
-                sprobe[pl.ds(r + 128 * half, 128), j * 128 : (j + 1) * 128] = hit
+                sprobe[pl.ds(r + 128 * side, 128), j * 128 : (j + 1) * 128] = hit
 
     looped(requests, pick_rows)
 
@@ -236,8 +272,8 @@
         hnp[rows, :] = dot(picked, nf[1, 0:512, :])
 
     unrolled(requests, pick_part)
-    for k in range(8):
-        halo_copy(1, k).wait_recv()
+    for c in range(2):
+        halo_share(1, c).wait_recv()
     edge_update(1)
 
     def probe_sums(c):
@@ -253,8 +289,13 @@
         rows = slice(2 * c * qslot, (2 * c + 2) * qslot)
         probe_exchange(c).wait_recv()
         probe_out[rows, :] = mlp(1, pick[rows, :], hnp[rows, :], mine[rows, :], theirs_in[rows, :])
-        probe_copy(2 * c).start()
-        probe_copy(2 * c + 1).start()
+        if c != 2:
+            probe_copy(2 * c).start()
+            probe_copy(2 * c + 1).start()
+            return
+        for k, sends, _ in relays:
+            pl.when(sends)(relay_out(k).start)
+            pl.when(jnp.logical_not(sends))(probe_copy(k).start)
 
     probe_sums(FAR_FIRST[0])
     probe_sums(FAR_FIRST[1])
@@ -269,6 +310,16 @@
     sum_edges(1, 1)
     node_lat_part(1, h1)
 
+    def pass_on(k):
+        def go():
+            relay_out(k).wait_recv()
+            relay_on(k).start()
+
+        return go
+
+    for k, _, passes in relays:
+        pl.when(passes)(pass_on(k))
+
     def interp_weights(r):
         here = sublanes + r
         for j in range(probes // 128):
@@ -294,14 +345,20 @@
 
     store.wait()
     index_copy.wait_send()
+    halo_exchange.wait_send()
     for k in range(8):
         halo_copy(0, k).wait_send()
         halo_copy(1, k).wait_send()
-        probe_copy(k).wait_send()
+        if k not in (4, 5):
+            probe_copy(k).wait_send()
+    for k, sends, passes in relays:
+        pl.when(sends)(relay_out(k).wait_send)
+        pl.when(jnp.logical_not(sends))(probe_copy(k).wait_send)
+        pl.when(passes)(relay_on(k).wait_send)
     for c in range(2):
-        exchange(0, c).wait_send()
-        exchange(1, c).wait_send()
-        halo_exchange(c).wait_send()
+        for layer in range(2):
+            exchange(layer, c).wait_send()
+            halo_share(layer, c).wait_send()
     for c in range(4):
         probe_exchange(c).wait_send()
 
@@ -346,24 +403,29 @@
     made = pl.pallas_call(
         kernel,
         out_shape=outs,
-        in_specs=[anywhere] * 2 + [vmem] * 6 + [anywhere] * 6 + [vmem],
+        in_specs=[anywhere] * 15,
         out_specs=(anywhere, vmem),
         scratch_shapes=[
+            buf(edges // 128, 128, dtype=i32), buf(edges // 128, 128, dtype=i32),
+            buf(*halo_rows.shape, dtype=i32), buf(*probe_rows.shape, dtype=i32),
+            buf(*probe_slot.shape[::-1], dtype=i32), buf(*probe_wgt.shape[::-1], dtype=F32), buf(*decode_second.shape),
             buf(nodes, width), buf(nodes, width), buf(nodes, width), buf(edges, width), buf(probes, width),
             buf(*edge_first.shape), buf(*edge_second.shape), buf(*node_first.shape), buf(*node_second.shape),
             buf(*decode_first.shape),
             buf(edges, 128, dtype=i32), buf(edges, 128, dtype=i32), buf(halos, 128, dtype=i32),
             buf(2 * requests, 128, dtype=i32), buf(*probe_rows.shape, dtype=i32),
-            buf(edges, nodes + halos), buf(edges, nodes), buf(nodes, edges), buf(halos, nodes), buf(halos, edges),
+            buf(edges, nodes + halos), buf(edges, nodes), buf(nodes, edges), buf(halos // 2, nodes), buf(halos, edges),
             buf(requests, nodes), buf(2 * requests, edges), buf(probes, requests),
             buf(edges, width), buf(edges, width, dtype=F32), buf(nodes, width, dtype=F32),
-            buf(halos, width, dtype=F32), buf(requests, width, dtype=F32),
-            buf(layers, nodes, width), buf(layers, nodes, width), buf(halos, width), buf(halos, width),
-            buf(layers, halos, width), buf(layers, halos, width),
+            buf(halos // 2, width, dtype=F32), buf(requests, width, dtype=F32),
+            buf(layers, nodes, width), buf(layers, nodes, width),
+            buf(halos // 2, width), buf(halos // 2, width), buf(halos // 2, width),
+            buf(layers, halos // 2, width), buf(layers, halos, width),
             buf(requests, width), buf(requests, width), buf(requests, width), buf(requests, width),
-            buf(requests, width), buf(requests, width),
-            dma((12,)), dma((1,)), dma((layers, 8)), dma((layers, 8)), dma((layers, 2)), dma((layers, 2)),
-            dma((2,)), dma((2,)), dma((4,)), dma((4,)), dma((8,)), dma((8,)), dma((1,)), dma((1,)),
+            buf(requests, width), buf(requests, width), buf(requests // 8, width),
+            dma((19,)), dma((1,)), dma((layers, 8)), dma((layers, 8)), dma((layers, 2)), dma((layers, 2)),
+            dma((1,)), dma((1,)), dma((4,)), dma((4,)), dma((8,)), dma((8,)), dma((1,)), dma((1,)),
+            dma((layers, 2)), dma((layers, 2)), dma((1,)), dma((1,)), dma((1,)),
         ],
         compiler_params=pltpu.CompilerParams(
             collective_id=0, has_side_effects=True, vmem_limit_bytes=60 * 1024 * 1024

time: 62.6 us -> 59.4 us (0.949)
  Pallas kernels: 61.6 us -> 58.3 us
    pallas_call x1, Pallas kernels: 59.6 us -> 56.3 us  [body(): pl.pallas_call(kernel, out_shape=outs, in_specs=[anywhere] * 15, out_spec...]
where the time goes in v2:
time: 59.4 us; the launch traced here: 59.1 us
  Pallas kernels  58.3 us (98%)
  between operations  0.8 us (1%)
    pallas_call x1, Pallas kernels, body(): pl.pallas_call(kernel, out_shape=outs, in_specs=[anywhere] * 15, out_spec...  56.3 us
    pallas_call x1, Pallas kernels, body(): pl.pallas_call(handover, out_shape=outs, in_specs=[anywhere] * 2, out_spe...  2.01 us

profile of v2, /device:TPU:1, one launch (start us, length us, event | category | flops | bytes accessed | tf_op | source)
XLA Modules:
  0.0 59.1 jit_solution(8733333480381876969)
XLA Ops:
  0.6 56.3 %shard_map.158 = (bf16[1024,512]{1,0:T(8,128)(2,1)}, f32[4,512]{1,0:T(4,128)}) custom-call(bf16[1024,512]{1,0:T(8,128)(2,1)} %node_hbm.1, bf16[1024,512]{1,0:T(8,128)(2,1)} %edge_hbm.1, s32[8,128]{1,0:T(8,128)} %bitcast.6, s32[8,128]{1,0:T(8,128)} %bitcast.7, s32[8,64]{1,0:T(8,128)} %hrows_hbm.1, s32[8,128]{1,0:T(8,128)} %prows_hbm.1, s32[8,512]{1,0:T(8,128)} %bitcast.4, ...), custom_call_target="tpu_custom_call" | custom-call | tf_op jit(solution)/shard_map/pallas_call | solution.py:403
  57.0 2.0 %shard_map.159 = (bf16[1024,512]{1,0:T(8,128)(2,1)}, f32[4,512]{1,0:T(4,128)}) custom-call(bf16[1024,512]{1,0:T(8,128)(2,1)} %get-tuple-element.4.surface, f32[4,512]{1,0:T(4,128)} %get-tuple-element.5.fields), custom_call_target="tpu_custom_call" | custom-call | tf_op jit(solution)/shard_map/pallas_call | solution.py:438

commit v3 on v2

--- a/solution.py
+++ b/solution.py
@@ -12,7 +12,7 @@
 OFFSETS = (1, -1, SPAN, -SPAN, SPAN + 1, -SPAN - 1, SPAN - 1, 1 - SPAN)
 ROWS = 512
 SEL = 256
-FAR_FIRST = (2, 3, 0, 1)
+PIECES = ((4, 1), (5, 1), (0, 2), (6, 2), (2, 2))
 
 
 def dot(a, b):
@@ -105,23 +105,38 @@
 
     halo_exchange = remote(halo_theirs, halo_theirs_in, ys_sem.at[0], yr_sem.at[0], (dom, peer))
 
-    def probe_exchange(c):
-        rows = pl.ds(c * 2 * qslot, 2 * qslot)
-        return remote(theirs.at[rows, :], theirs_in.at[rows, :], zs_sem.at[c], zr_sem.at[c], (dom, peer))
+    def probe_exchange(i):
+        rows = pl.ds(PIECES[i][0] * qslot, PIECES[i][1] * qslot)
+        return remote(theirs.at[rows, :], theirs_in.at[rows, :], zs_sem.at[i], zr_sem.at[i], (dom, peer))
 
     def probe_copy(k):
         rows = pl.ds(k * qslot, qslot)
         return remote(probe_out.at[rows, :], probe_in.at[rows, :], ps_sem.at[k], pr_sem.at[k], (targets[k], feat))
 
-    def relay_out(k):
+    even = feat == 0
+    relays = (
+        (4, is_last, is_first, 0, 2, 0),
+        (5, is_first, is_last, 1, 3, 0),
+        (0, jnp.logical_and(is_last, even), jnp.logical_and(is_first, even), 7, 2, 1),
+        (1, jnp.logical_and(is_first, even), jnp.logical_and(is_last, even), 6, 3, 1),
+    )
+
+    def relay_out(k, via, i):
         rows = pl.ds(k * qslot, qslot)
-        return remote(probe_out.at[rows, :], relay_in, rs_sem.at[0], rr_sem.at[0], (targets[k - 4], feat))
-
-    def relay_on(k):
+        return remote(probe_out.at[rows, :], relay_in.at[i], rs_sem.at[i], rr_sem.at[i], (targets[via], feat))
+
+    def relay_on(k, on, i):
         rows = pl.ds(k * qslot, qslot)
-        return remote(relay_in, probe_in.at[rows, :], gs_sem.at[0], pr_sem.at[k], (targets[k - 2], feat))
-
-    relays = ((4, is_last, is_first), (5, is_first, is_last))
+        return remote(relay_in.at[i], probe_in.at[rows, :], gs_sem.at[i], pr_sem.at[k], (targets[on], feat))
+
+    def pass_on(buffer):
+        for k, _, passes, via, on, i in relays:
+            if i == buffer:
+
+                @pl.when(passes)
+                def _():
+                    relay_out(k, via, i).wait_recv()
+                    relay_on(k, on, i).start()
 
     index_copy = remote(prows, prows_in, is_sem.at[0], ir_sem.at[0], (dom, peer))
 
@@ -205,11 +220,10 @@
         part[layer, rows, :] = dot(tdst[rows, :], edge[...]).astype(BF)
         exchange(layer, c).start()
 
-    def node_update(layer, h, new):
-        for c in range(nodes // ROWS):
-            rows = slice(c * ROWS, (c + 1) * ROWS)
-            exchange(layer, c).wait_recv()
-            new[rows, :] = mlp(layer, h[rows, :], hn[rows, :], part[layer, rows, :], part_in[layer, rows, :])
+    def node_update(layer, h, new, c):
+        rows = slice(c * ROWS, (c + 1) * ROWS)
+        exchange(layer, c).wait_recv()
+        new[rows, :] = mlp(layer, h[rows, :], hn[rows, :], part[layer, rows, :], part_in[layer, rows, :])
 
     def share_halo(layer):
         for c in range(2):
@@ -252,10 +266,7 @@
     for load in loads[10:]:
         load.wait()
     edge_lat_part(1)
-    node_update(0, h0, h1)
-
-    own_part(1, h1)
-    share_halo(1)
+    node_update(0, h0, h1, 0)
 
     def pick_rows(r):
         for side in range(2):
@@ -265,60 +276,62 @@
                 sprobe[pl.ds(r + 128 * side, 128), j * 128 : (j + 1) * 128] = hit
 
     looped(requests, pick_rows)
+    node_update(0, h0, h1, 1)
+
+    own_part(1, h1)
+    share_halo(1)
 
     def pick_part(rows):
         picked = dot(sprobe[rows, :], h1[...]).astype(BF)
         pick[rows, :] = picked
         hnp[rows, :] = dot(picked, nf[1, 0:512, :])
 
-    unrolled(requests, pick_part)
+    pick_part(slice(4 * qslot, 6 * qslot))
+    pick_part(slice(0, 4 * qslot))
     for c in range(2):
         halo_share(1, c).wait_recv()
     edge_update(1)
 
-    def probe_sums(c):
-        here = 4 * qslot * c
-        both = dot(tprobe[here : here + 4 * qslot, :], edge[...]).astype(BF)
-        for i in range(2):
-            rows = slice((2 * c + i) * qslot, (2 * c + i + 1) * qslot)
-            theirs[rows, :] = both[2 * i * qslot : (2 * i + 1) * qslot]
-            mine[rows, :] = both[(2 * i + 1) * qslot : (2 * i + 2) * qslot]
-        probe_exchange(c).start()
-
-    def probe_rows(c):
-        rows = slice(2 * c * qslot, (2 * c + 2) * qslot)
-        probe_exchange(c).wait_recv()
+    def probe_sums(i):
+        first, number = PIECES[i]
+        both = dot(tprobe[2 * first * qslot : 2 * (first + number) * qslot, :], edge[...]).astype(BF)
+        for n in range(number):
+            rows = slice((first + n) * qslot, (first + n + 1) * qslot)
+            theirs[rows, :] = both[2 * n * qslot : (2 * n + 1) * qslot]
+            mine[rows, :] = both[(2 * n + 1) * qslot : (2 * n + 2) * qslot]
+        probe_exchange(i).start()
+
+    def probe_rows(i):
+        first, number = PIECES[i]
+        rows = slice(first * qslot, (first + number) * qslot)
+        probe_exchange(i).wait_recv()
         probe_out[rows, :] = mlp(1, pick[rows, :], hnp[rows, :], mine[rows, :], theirs_in[rows, :])
-        if c != 2:
-            probe_copy(2 * c).start()
-            probe_copy(2 * c + 1).start()
-            return
-        for k, sends, _ in relays:
-            pl.when(sends)(relay_out(k).start)
-            pl.when(jnp.logical_not(sends))(probe_copy(k).start)
-
-    probe_sums(FAR_FIRST[0])
-    probe_sums(FAR_FIRST[1])
-    probe_rows(FAR_FIRST[0])
-    probe_sums(FAR_FIRST[2])
-    probe_rows(FAR_FIRST[1])
-    probe_sums(FAR_FIRST[3])
-    probe_rows(FAR_FIRST[2])
-    probe_rows(FAR_FIRST[3])
+        for k in range(first, first + number):
+            relayed = [relay for relay in relays if relay[0] == k]
+            for _, sends, _, via, _, i in relayed:
+                pl.when(sends)(relay_out(k, via, i).start)
+                pl.when(jnp.logical_not(sends))(probe_copy(k).start)
+            if not relayed:
+                probe_copy(k).start()
+
+    probe_sums(0)
+    probe_sums(1)
+    probe_sums(2)
+    probe_rows(0)
+    probe_rows(1)
+    probe_sums(3)
+    probe_rows(2)
+    pick_part(slice(6 * qslot, 8 * qslot))
+    probe_sums(4)
+    probe_rows(3)
+    probe_rows(4)
+    pass_on(0)
 
     sum_edges(1, 0)
     sum_edges(1, 1)
     node_lat_part(1, h1)
 
-    def pass_on(k):
-        def go():
-            relay_out(k).wait_recv()
-            relay_on(k).start()
-
-        return go
-
-    for k, _, passes in relays:
-        pl.when(passes)(pass_on(k))
+    pass_on(1)
 
     def interp_weights(r):
         here = sublanes + r
@@ -330,12 +343,13 @@
             wint[j * 128 : (j + 1) * 128, pl.ds(r, SEL)] = jnp.transpose(total).astype(BF)
 
     looped(requests, interp_weights)
-    node_update(1, h1, h2)
+    node_update(1, h1, h2, 0)
+    node_update(1, h1, h2, 1)
     store = pltpu.make_async_copy(h2, out_hbm, store_sem.at[0])
     store.start()
 
     total = emb[...].astype(F32)
-    for c in FAR_FIRST:
+    for c in (1, 3, 0, 2):
         rows = slice(2 * c * qslot, (2 * c + 2) * qslot)
         probe_copy(2 * c).wait_recv()
         probe_copy(2 * c + 1).wait_recv()
@@ -349,24 +363,25 @@
     for k in range(8):
         halo_copy(0, k).wait_send()
         halo_copy(1, k).wait_send()
-        if k not in (4, 5):
+        relayed = [relay for relay in relays if relay[0] == k]
+        for _, sends, passes, via, on, i in relayed:
+            pl.when(sends)(relay_out(k, via, i).wait_send)
+            pl.when(jnp.logical_not(sends))(probe_copy(k).wait_send)
+            pl.when(passes)(relay_on(k, on, i).wait_send)
+        if not relayed:
             probe_copy(k).wait_send()
-    for k, sends, passes in relays:
-        pl.when(sends)(relay_out(k).wait_send)
-        pl.when(jnp.logical_not(sends))(probe_copy(k).wait_send)
-        pl.when(passes)(relay_on(k).wait_send)
     for c in range(2):
         for layer in range(2):
             exchange(layer, c).wait_send()
             halo_share(layer, c).wait_send()
-    for c in range(4):
-        probe_exchange(c).wait_send()
+    for i in range(len(PIECES)):
+        probe_exchange(i).wait_send()
 
 
 def handover(surface, fields, surface_out, fields_out, rows, line, in_sem, out_sem):
-    part = surface.shape[0] // 4
+    part = surface.shape[0] // 8
     pieces = [(fields, line, fields_out)]
-    for i in range(4):
+    for i in range(8):
         cut = pl.ds(i * part, part)
         pieces.append((surface.at[cut, :], rows.at[cut, :], surface_out.at[cut, :]))
     ins = [pltpu.make_async_copy(src, mid, in_sem.at[i]) for i, (src, mid, _) in enumerate(pieces)]
@@ -422,10 +437,10 @@
             buf(halos // 2, width), buf(halos // 2, width), buf(halos // 2, width),
             buf(layers, halos // 2, width), buf(layers, halos, width),
             buf(requests, width), buf(requests, width), buf(requests, width), buf(requests, width),
-            buf(requests, width), buf(requests, width), buf(requests // 8, width),
+            buf(requests, width), buf(requests, width), buf(2, requests // 8, width),
             dma((19,)), dma((1,)), dma((layers, 8)), dma((layers, 8)), dma((layers, 2)), dma((layers, 2)),
-            dma((1,)), dma((1,)), dma((4,)), dma((4,)), dma((8,)), dma((8,)), dma((1,)), dma((1,)),
-            dma((layers, 2)), dma((layers, 2)), dma((1,)), dma((1,)), dma((1,)),
+            dma((1,)), dma((1,)), dma((5,)), dma((5,)), dma((8,)), dma((8,)), dma((1,)), dma((1,)),
+            dma((layers, 2)), dma((layers, 2)), dma((2,)), dma((2,)), dma((2,)),
         ],
         compiler_params=pltpu.CompilerParams(
             collective_id=0, has_side_effects=True, vmem_limit_bytes=60 * 1024 * 1024
@@ -440,7 +455,7 @@
         out_shape=outs,
         in_specs=[anywhere] * 2,
         out_specs=(anywhere, anywhere),
-        scratch_shapes=[buf(nodes, width), buf(fields, probes, dtype=F32), dma((5,)), dma((5,))],
+        scratch_shapes=[buf(nodes, width), buf(fields, probes, dtype=F32), dma((9,)), dma((9,))],
     )(*made)
 
 

time: 59.4 us -> 58.5 us (0.985)
  Pallas kernels: 58.3 us -> 57.5 us
    pallas_call x1, Pallas kernels: 56.3 us -> 55.4 us  [body(): pl.pallas_call(kernel, out_shape=outs, in_specs=[anywhere] * 15, out_spec...]
where the time goes in v3:
time: 58.5 us; the launch traced here: 58.3 us
  Pallas kernels  57.5 us (98%)
  between operations  0.82 us (1%)
    pallas_call x1, Pallas kernels, body(): pl.pallas_call(kernel, out_shape=outs, in_specs=[anywhere] * 15, out_spec...  55.4 us
    pallas_call x1, Pallas kernels, body(): pl.pallas_call(handover, out_shape=outs, in_specs=[anywhere] * 2, out_spe...  2.12 us

profile of v3, /device:TPU:1, one launch (start us, length us, event | category | flops | bytes accessed | tf_op | source)
XLA Modules:
  0.0 58.3 jit_solution(3162640254512985507)
XLA Ops:
  0.6 55.4 %shard_map.158 = (bf16[1024,512]{1,0:T(8,128)(2,1)}, f32[4,512]{1,0:T(4,128)}) custom-call(bf16[1024,512]{1,0:T(8,128)(2,1)} %node_hbm.1, bf16[1024,512]{1,0:T(8,128)(2,1)} %edge_hbm.1, s32[8,128]{1,0:T(8,128)} %bitcast.6, s32[8,128]{1,0:T(8,128)} %bitcast.7, s32[8,64]{1,0:T(8,128)} %hrows_hbm.1, s32[8,128]{1,0:T(8,128)} %prows_hbm.1, s32[8,512]{1,0:T(8,128)} %bitcast.4, ...), custom_call_target="tpu_custom_call" | custom-call | tf_op jit(solution)/shard_map/pallas_call | solution.py:418
  56.0 2.1 %shard_map.159 = (bf16[1024,512]{1,0:T(8,128)(2,1)}, f32[4,512]{1,0:T(4,128)}) custom-call(bf16[1024,512]{1,0:T(8,128)(2,1)} %get-tuple-element.4.surface, f32[4,512]{1,0:T(4,128)} %get-tuple-element.5.fields), custom_call_target="tpu_custom_call" | custom-call | tf_op jit(solution)/shard_map/pallas_call | solution.py:453

commit v4 on v3

--- a/solution.py
+++ b/solution.py
@@ -46,12 +46,12 @@
 def kernel(
     node_hbm, edge_hbm, esrc_hbm, edst_hbm, hrows_hbm, prows_hbm, pslot_hbm, pwgt_hbm, emb_hbm,
     ef_hbm, es_hbm, nf_hbm, ns_hbm, d1_hbm, d2_hbm,
-    out_hbm, fields,
-    esrc, edst, hrows, prows, pslot, pwgt, d2, h0, h1, h2, edge, emb, ef, es, nf, ns, d1,
+    h2, fields,
+    esrc, edst, hrows, prows, pslot, pwgt, d2, h0, h1, edge, emb, ef, es, nf, ns, d1,
     csrc, cdst, chalo, cprobe, prows_in, ssrc, sdst, tdst, shalo, thalo, sprobe, tprobe, wint,
     own, pre, hn, hnh, hnp, part, part_in, halo_mine, halo_theirs, halo_theirs_in, halo_out, halo_in,
     pick, mine, theirs, theirs_in, probe_out, probe_in, relay_in,
-    load_sem, store_sem, hs_sem, hr_sem, xs_sem, xr_sem, ys_sem, yr_sem, zs_sem, zr_sem, ps_sem, pr_sem, is_sem, ir_sem,
+    load_sem, hs_sem, hr_sem, xs_sem, xr_sem, ys_sem, yr_sem, zs_sem, zr_sem, ps_sem, pr_sem, is_sem, ir_sem,
     fs_sem, fr_sem, rs_sem, rr_sem, gs_sem,
 ):
     nodes, edges = h0.shape[0], edge.shape[0]
@@ -117,8 +117,6 @@
     relays = (
         (4, is_last, is_first, 0, 2, 0),
         (5, is_first, is_last, 1, 3, 0),
-        (0, jnp.logical_and(is_last, even), jnp.logical_and(is_first, even), 7, 2, 1),
-        (1, jnp.logical_and(is_first, even), jnp.logical_and(is_last, even), 6, 3, 1),
     )
 
     def relay_out(k, via, i):
@@ -331,7 +329,6 @@
     sum_edges(1, 1)
     node_lat_part(1, h1)
 
-    pass_on(1)
 
     def interp_weights(r):
         here = sublanes + r
@@ -345,8 +342,6 @@
     looped(requests, interp_weights)
     node_update(1, h1, h2, 0)
     node_update(1, h1, h2, 1)
-    store = pltpu.make_async_copy(h2, out_hbm, store_sem.at[0])
-    store.start()
 
     total = emb[...].astype(F32)
     for c in (1, 3, 0, 2):
@@ -357,7 +352,6 @@
     hidden = jnp.maximum(dot(total.astype(BF), d1[...]), 0.0).astype(BF)
     fields[...] = lax.dot_general(d2[...], hidden, (((1,), (1,)), ((), ())), preferred_element_type=F32)
 
-    store.wait()
     index_copy.wait_send()
     halo_exchange.wait_send()
     for k in range(8):
@@ -378,21 +372,16 @@
         probe_exchange(i).wait_send()
 
 
-def handover(surface, fields, surface_out, fields_out, rows, line, in_sem, out_sem):
-    part = surface.shape[0] // 8
-    pieces = [(fields, line, fields_out)]
-    for i in range(8):
+def handover(surface, fields, surface_out, fields_out, sem):
+    part = surface.shape[0] // 4
+    moves = [pltpu.make_async_copy(fields, fields_out, sem.at[4])]
+    for i in range(4):
         cut = pl.ds(i * part, part)
-        pieces.append((surface.at[cut, :], rows.at[cut, :], surface_out.at[cut, :]))
-    ins = [pltpu.make_async_copy(src, mid, in_sem.at[i]) for i, (src, mid, _) in enumerate(pieces)]
-    outs = [pltpu.make_async_copy(mid, dst, out_sem.at[i]) for i, (_, mid, dst) in enumerate(pieces)]
-    for move in ins:
+        moves.append(pltpu.make_async_copy(surface.at[cut, :], surface_out.at[cut, :], sem.at[i]))
+    for move in moves:
         move.start()
-    for move, onward in zip(ins, outs):
+    for move in moves:
         move.wait()
-        onward.start()
-    for onward in outs:
-        onward.wait()
 
 
 def body(
@@ -406,25 +395,20 @@
     anywhere = pl.BlockSpec(memory_space=pl.ANY)
     vmem = pl.BlockSpec(memory_space=pltpu.VMEM)
     dma = pltpu.SemaphoreType.DMA
-    outs = (
-        jax.ShapeDtypeStruct((nodes, width), BF),
-        jax.ShapeDtypeStruct((fields, probes), F32),
-    )
-
     def buf(*shape, dtype=BF):
         return pltpu.VMEM(shape, dtype)
 
     i32 = jnp.int32
     made = pl.pallas_call(
         kernel,
-        out_shape=outs,
+        out_shape=(pltpu.VMEM((nodes, width), BF), pltpu.VMEM((fields, probes), F32)),
         in_specs=[anywhere] * 15,
-        out_specs=(anywhere, vmem),
+        out_specs=(vmem, vmem),
         scratch_shapes=[
             buf(edges // 128, 128, dtype=i32), buf(edges // 128, 128, dtype=i32),
             buf(*halo_rows.shape, dtype=i32), buf(*probe_rows.shape, dtype=i32),
             buf(*probe_slot.shape[::-1], dtype=i32), buf(*probe_wgt.shape[::-1], dtype=F32), buf(*decode_second.shape),
-            buf(nodes, width), buf(nodes, width), buf(nodes, width), buf(edges, width), buf(probes, width),
+            buf(nodes, width), buf(nodes, width), buf(edges, width), buf(probes, width),
             buf(*edge_first.shape), buf(*edge_second.shape), buf(*node_first.shape), buf(*node_second.shape),
             buf(*decode_first.shape),
             buf(edges, 128, dtype=i32), buf(edges, 128, dtype=i32), buf(halos, 128, dtype=i32),
@@ -438,7 +422,7 @@
             buf(layers, halos // 2, width), buf(layers, halos, width),
             buf(requests, width), buf(requests, width), buf(requests, width), buf(requests, width),
             buf(requests, width), buf(requests, width), buf(2, requests // 8, width),
-            dma((19,)), dma((1,)), dma((layers, 8)), dma((layers, 8)), dma((layers, 2)), dma((layers, 2)),
+            dma((19,)), dma((layers, 8)), dma((layers, 8)), dma((layers, 2)), dma((layers, 2)),
             dma((1,)), dma((1,)), dma((5,)), dma((5,)), dma((8,)), dma((8,)), dma((1,)), dma((1,)),
             dma((layers, 2)), dma((layers, 2)), dma((2,)), dma((2,)), dma((2,)),
         ],
@@ -450,12 +434,13 @@
         probe_slot.T, probe_wgt.T, probe_embed,
         edge_first, edge_second, node_first, node_second, decode_first, decode_second,
     )
+    made = [pltpu.with_memory_space_constraint(array, pltpu.VMEM) for array in made]
     return pl.pallas_call(
         handover,
-        out_shape=outs,
-        in_specs=[anywhere] * 2,
+        out_shape=(jax.ShapeDtypeStruct((nodes, width), BF), jax.ShapeDtypeStruct((fields, probes), F32)),
+        in_specs=[vmem] * 2,
         out_specs=(anywhere, anywhere),
-        scratch_shapes=[buf(nodes, width), buf(fields, probes, dtype=F32), dma((9,)), dma((9,))],
+        scratch_shapes=[dma((5,))],
     )(*made)
 
 

time: 58.5 us -> 56.7 us (0.969)
  Pallas kernels: 57.5 us -> 55.8 us
    pallas_call x2, Pallas kernels: 57.5 us -> 55.8 us  [the longest x1 54.8 us: body(): pl.pallas_call(kernel, out_shape=(pltpu.VMEM((nodes, width), BF), pltpu.V...]
where the time goes in v4:
time: 56.7 us; the launch traced here: 56.6 us
  Pallas kernels  55.8 us (98%)
  between operations  0.82 us (1%)
    pallas_call x1, Pallas kernels, body(): pl.pallas_call(kernel, out_shape=(pltpu.VMEM((nodes, width), BF), pltpu.V...  54.8 us

profile of v4, /device:TPU:1, one launch (start us, length us, event | category | flops | bytes accessed | tf_op | source)
XLA Modules:
  0.0 56.6 jit_solution(11283058899137209865)
XLA Ops:
  0.6 54.8 %shard_map.158 = (bf16[1024,512]{1,0:T(8,128)(2,1)S(1)}, f32[4,512]{1,0:T(4,128)S(1)}) custom-call(bf16[1024,512]{1,0:T(8,128)(2,1)} %node_hbm.1, bf16[1024,512]{1,0:T(8,128)(2,1)} %edge_hbm.1, s32[8,128]{1,0:T(8,128)} %bitcast.6, s32[8,128]{1,0:T(8,128)} %bitcast.7, s32[8,64]{1,0:T(8,128)} %hrows_hbm.1, s32[8,128]{1,0:T(8,128)} %prows_hbm.1, ...), custom_call_target="tpu_custom_call" | custom-call | tf_op jit(solution)/shard_map/pallas_call | solution.py:402
  55.4 1.0 %shard_map.159 = (bf16[1024,512]{1,0:T(8,128)(2,1)}, f32[4,512]{1,0:T(4,128)}) custom-call(bf16[1024,512]{1,0:T(8,128)(2,1)S(1)} %get-tuple-element.4.surface, f32[4,512]{1,0:T(4,128)S(1)} %get-tuple-element.5.fields), custom_call_target="tpu_custom_call" | custom-call | tf_op jit(solution)/shard_map/pallas_call | solution.py:438
